TPU v7x, 768 devices: a whole 4x8x12 slice. The times are simulated.
768 devices in a mesh: blk: 384 (over x, z, y), rep: 2 (over core).
Axes of the slice: x: 4, y: 8, z: 12, core: 2. Of those that a mesh axis runs over, the one named last changes fastest.
Arguments:
- features: bfloat16 [786432, 256], P('blk', 'rep'), may hold values from -0.0068359375 to 0.0068359375
- out_grad: bfloat16 [786432, 256], P('blk', 'rep'), may hold values from -6 to 6
- block_tiles: bfloat16 [24576, 128, 128], P('blk'), may hold values from -0.25 to 0.25
- block_cols: int32 [24576], P('blk'), may hold values from 0 to 6143, as said below
- self_weight: bfloat16 [256, 256], P('rep'), may hold values from -0.375 to 0.375
- neighbor_weight: bfloat16 [256, 256], P('rep'), may hold values from -0.375 to 0.375
Outputs:
- feature_grad: float32 [786432, 256], P('blk', 'rep')
- self_weight_grad: float32 [256, 256], P('rep')
- neighbor_weight_grad: float32 [256, 256], P('rep')
Inputs may be any that keep to these rules, and one draw needn't show every extreme that they name: `block_cols`: slots m * 64 to (m + 1) * 64 - 1 hold the tiles of row blocks m * 16 to (m + 1) * 16 - 1 (range m). Every tile names a column block of its own range, except the first tile of row block m * 16 + b: for b < 2 it names block 15 - b of range m - 1, for b >= 14 block 15 - b of range m + 1, where range -1 is the last range and the range after the last is range 0.
All inputs are finite; a program needn't handle non-finite values.
Results may differ from a plain program's by a relative error of at most 0.0031.
Values may be sent and summed in bfloat16 or wider, within the bound.
A program may use at most 32 MiB of HBM per device.

v0:
```python
import jax
import jax.numpy as jnp
from jax import lax
from jax.sharding import PartitionSpec as P

HALO = 2


def padded(shard, sides, width):
    for axis, dim in sides:
        size, length = (lax.axis_size(axis), shard.shape[dim])
        up = [(i, (i + 1) % size) for i in range(size)]
        down = [(j, i) for i, j in up]
        last = lax.slice_in_dim(shard, length - width, length, axis=dim)
        initial = lax.slice_in_dim(shard, 0, width, axis=dim)
        before = lax.ppermute(last, axis, up)
        after = lax.ppermute(initial, axis, down)
        shard = jnp.concatenate([before, shard, after], axis=dim)
    return shard


def passed_along(block, axis, distance):
    devices = range(lax.axis_size(axis))
    route = [((i - distance) % len(devices), i) for i in devices]
    return lax.ppermute(block, axis, route)


def body(features, out_grad, block_tiles, block_cols, self_weight, neighbor_weight):
    row_count, columns = features.shape
    tile_side = block_tiles.shape[1]
    block_count = row_count // tile_side
    tiles_per = block_tiles.shape[0] // block_count
    all_blocks = block_count * lax.axis_size("blk")
    first_block = lax.axis_index("blk") * block_count
    rim_rows = HALO * tile_side
    full_grad = lax.all_gather(out_grad, "rep", axis=1, tiled=True)
    tile_grid = block_tiles.reshape(block_count, tiles_per, tile_side, tile_side)
    extended = padded(features, (("blk", 0),), rim_rows)
    window_blocks = extended.reshape(block_count + 2 * HALO, tile_side, columns)
    window_slot = (block_cols - first_block + HALO) % all_blocks
    picked = jnp.take(window_blocks, window_slot, axis=0)
    forward = jnp.einsum("tij,tjk->tik", block_tiles, picked, preferred_element_type=jnp.float32)
    aggregate = (
        forward.reshape(block_count, tiles_per, tile_side, columns)
        .sum(axis=1)
        .reshape(row_count, columns)
        .astype(jnp.bfloat16)
    )
    contract = (((1,), (1,)), ((), ()))
    projected = lax.dot_general(
        full_grad, neighbor_weight, contract, preferred_element_type=jnp.float32
    ).astype(jnp.bfloat16)
    self_term = lax.dot_general(
        full_grad, self_weight, contract, preferred_element_type=jnp.float32
    )
    proj_blocks = projected.reshape(block_count, tile_side, columns)
    backward = jnp.einsum(
        "bpij,bik->bpjk", tile_grid, proj_blocks, preferred_element_type=jnp.float32
    )
    backward = backward.reshape(block_count * tiles_per, tile_side * columns)
    window_ids = jnp.arange(block_count + 2 * HALO, dtype=jnp.int32)
    onehot = (window_slot[None, :] == window_ids[:, None]).astype(jnp.float32)
    summed = jnp.dot(onehot, backward, precision=lax.Precision.HIGHEST).reshape(
        block_count + 2 * HALO, tile_side, columns
    )
    neighbor = summed[HALO : HALO + block_count]
    for offset in (-1, 1):
        border = summed[:HALO] if offset == -1 else summed[HALO + block_count :]
        arrived = passed_along(border, "blk", offset)
        if offset == -1:
            neighbor = neighbor.at[block_count - HALO :].add(arrived)
        else:
            neighbor = neighbor.at[:HALO].add(arrived)
    feature_grad = self_term + neighbor.reshape(row_count, columns)
    rows_contract = (((0,), (0,)), ((), ()))
    self_part = lax.dot_general(
        features, full_grad, rows_contract, preferred_element_type=jnp.float32
    )
    neighbor_part = lax.dot_general(
        aggregate, full_grad, rows_contract, preferred_element_type=jnp.float32
    )
    self_weight_grad, neighbor_weight_grad = lax.psum((self_part, neighbor_part), "blk")
    return (feature_grad, self_weight_grad, neighbor_weight_grad)


def solution(mesh):
    in_specs = (
        P("blk", "rep"),
        P("blk", "rep"),
        P("blk", None, None),
        P("blk"),
        P("rep", None),
        P("rep", None),
    )
    out_specs = (P("blk", "rep"), P("rep", None), P("rep", None))
    return jax.shard_map(body, mesh=mesh, in_specs=in_specs, out_specs=out_specs, check_vma=False)
```

profile of v0, /device:TPU:26, one launch (start us, length us, event | category | flops | bytes accessed | tf_op | source)
XLA Modules:
  0.0 456.6 jit_solution(1702118753039599076)
XLA Ops:
  7.2 0.7 all-gather.2.cloned.1.call-update
  8.0 0.9 fusion.13
  8.8 4.7 %collective-permute-start.2 = (bf16[256,128]{1,0:T(8,128)(2,1)S(1)}, bf16[256,128]{1,0:T(8,128)(2,1)S(1)}, u32[]{:S(2)}, u32[]{:S(2)}) collective-permute-start(bf16[256,128]{1,0:T(8,128)(2,1)S(1)} %get-tuple-element.34), channel_id=1, source_target_pairs={{0,2},{2,4},{4,6},{6,8},{8,10},{10,12},{12,14},{14,16},{16,18},{18... | collective-permute-start | bytes 196616 | tf_op jit(solution)/shard_map/ppermute | solution.py:16
  13.6 1.9 collective-permute-start.3
  16.2 4.7 %collective-permute-done.3 = bf16[256,128]{1,0:T(8,128)(2,1)S(1)} collective-permute-done((bf16[256,128]{1,0:T(8,128)(2,1)S(1)}, bf16[256,128]{1,0:T(8,128)(2,1)S(1)}, u32[]{:S(2)}, u32[]{:S(2)}) %collective-permute-start.3) | collective-permute-done | bytes 65568 | tf_op jit(solution)/shard_map/ppermute | solution.py:17
  20.9 1.1 pad_maximum_fusion
  22.0 2.2 gather_fusion
  24.2 3.4 bitcast_reduce_fusion
  27.6 1.0 copy.19
  28.6 8.1 %all-gather.2.cloned.1.call-done = bf16[2048,256]{1,0:T(8,128)(2,1)} async-done(((bf16[2048,128]{1,0:T(8,128)(2,1)}), bf16[2048,256]{1,0:T(8,128)(2,1)}) %all-gather.2.cloned.1.call-update) | async-done | bytes 1048592 | tf_op jit(solution)/shard_map/all_gather | solution.py:36
  36.7 1.6 convolution_convert_fusion
  38.4 2.7 convolution_bitcast_fusion
  41.1 5.4 %copy.17 = f32[16,4,128,128]{3,2,1,0:T(8,128)} copy(f32[16,4,128,128]{2,3,1,0:T(8,128)} %convolution_bitcast_fusion) | data formatting | bytes 8388608 | tf_op jit(solution)/shard_map/bpij,bik->bpjk/dot_general | solution.py:57
  46.5 5.9 %fusion = f32[20,16384]{1,0:T(8,128)S(1)} fusion(f32[8,8,128,128]{3,2,1,0:T(8,128)} %bitcast.52, s32[64]{0:T(128)S(1)} %get-tuple-element.30), kind=kOutput, calls=%fused_computation.1 | convolution fusion | flops 251659520 | bytes 5505280 | tf_op jit(solution)/shard_map/dot_general | solution.py:63
  53.3 2.6 collective-permute-start
  55.8 1.2 copy.25
  57.7 4.6 %collective-permute-start.1 = (f32[2,128,128]{2,1,0:T(8,128)}, f32[2,128,128]{2,1,0:T(8,128)S(1)}, u32[]{:S(2)}, u32[]{:S(2)}) collective-permute-start(f32[2,128,128]{2,1,0:T(8,128)} %bitcast.49), channel_id=1, source_target_pairs={{766,0},{0,2},{2,4},{4,6},{6,8},{8,10},{10,12},{12,14},{14,16},{16... | collective-permute-start | bytes 393224 | tf_op jit(solution)/shard_map/ppermute | solution.py:25
  62.3 1.0 fusion.14
  63.3 1.0 fusion.15
  65.5 1.6 fusion.10
  67.1 2.7 bitcast_add_fusion
  69.7 376.9 %all-reduce.3.cloned.1.call-done = (f32[128,256]{1,0:T(8,128)}, f32[128,256]{1,0:T(8,128)}) async-done(((f32[128,256]{1,0:T(8,128)}, f32[128,256]{1,0:T(8,128)}), (f32[128,256]{1,0:T(8,128)}, f32[128,256]{1,0:T(8,128)})) %all-reduce.3.cloned.1.call-update) | async-done | bytes 262160 | tf_op jit(solution)/shard_map/psum | solution.py:82
  446.6 1.6 copy.42
  448.2 1.6 copy.43
  (24 shorter events, 3.5 us)
Async XLA Ops:
  7.2 17.0 %copy-start = (bf16[64,128,128]{2,1,0:T(8,128)(2,1)S(1)}, bf16[64,128,128]{2,1,0:T(8,128)(2,1)}, u32[]{:S(2)}) copy-start(bf16[64,128,128]{2,1,0:T(8,128)(2,1)} %param.12) | copy-start | bytes 6291460
  7.2 29.6 %all-gather.2.cloned.1.call-start = ((), (), s32[]{:S(2)}) async-start(), calls=%async_computation | async-start | bytes 1572864 | tf_op jit(solution)/shard_map/all_gather | solution.py:36
  7.9 438.7 %all-reduce.3.cloned.1.call-start = ((), (), s32[]{:S(2)}) async-start(), calls=%async_computation.1 | async-start | bytes 524288 | tf_op jit(solution)/shard_map/psum | solution.py:82
  8.8 7.3 %collective-permute-start.2 = (bf16[256,128]{1,0:T(8,128)(2,1)S(1)}, bf16[256,128]{1,0:T(8,128)(2,1)S(1)}, u32[]{:S(2)}, u32[]{:S(2)}) collective-permute-start(bf16[256,128]{1,0:T(8,128)(2,1)S(1)} %get-tuple-element.34), channel_id=1, source_target_pairs={{0,2},{2,4},{4,6},{6,8},{8,10},{10,12},{12,14},{14,16},{16,18},{18... | collective-permute-start | bytes 196616 | tf_op jit(solution)/shard_map/ppermute | solution.py:16
  13.6 7.4 %collective-permute-start.3 = (bf16[256,128]{1,0:T(8,128)(2,1)S(1)}, bf16[256,128]{1,0:T(8,128)(2,1)S(1)}, u32[]{:S(2)}, u32[]{:S(2)}) collective-permute-start(bf16[256,128]{1,0:T(8,128)(2,1)S(1)} %get-tuple-element.35), channel_id=1, source_target_pairs={{2,0},{4,2},{6,4},{8,6},{10,8},{12,10},{14,12},{16,14},{18,16},{20... | collective-permute-start | bytes 196616 | tf_op jit(solution)/shard_map/ppermute | solution.py:17
  24.2 12.6 %copy-start.4 = (bf16[128,256]{1,0:T(8,128)(2,1)S(1)}, bf16[128,256]{1,0:T(8,128)(2,1)}, u32[]{:S(2)}) copy-start(bf16[128,256]{1,0:T(8,128)(2,1)} %param.15) | copy-start | bytes 196612
  52.5 9.8 %copy-start.1 = (bf16[2048,256]{1,0:T(8,128)(2,1)S(1)}, bf16[2048,256]{1,0:T(8,128)(2,1)}, u32[]{:S(2)}) copy-start(bf16[2048,256]{1,0:T(8,128)(2,1)} %all-gather.2.cloned.1.call-done) | copy-start | bytes 3145732
  52.5 9.8 %copy-start.2 = (bf16[2048,128]{1,0:T(8,128)(2,1)S(1)}, bf16[2048,128]{1,0:T(8,128)(2,1)}, u32[]{:S(2)}) copy-start(bf16[2048,128]{1,0:T(8,128)(2,1)} %param.10) | copy-start | bytes 1572868
  53.3 10.1 %copy-start.3 = (bf16[16,128,128]{2,1,0:T(8,128)(2,1)S(1)}, bf16[16,128,128]{2,1,0:T(8,128)(2,1)}, u32[]{:S(2)}) copy-start(bf16[16,128,128]{2,1,0:T(8,128)(2,1)} %copy.19) | copy-start | bytes 1572868
  53.3 11.1 %collective-permute-start = (f32[2,128,128]{2,1,0:T(8,128)}, f32[2,128,128]{2,1,0:T(8,128)S(1)}, u32[]{:S(2)}, u32[]{:S(2)}) collective-permute-start(f32[2,128,128]{2,1,0:T(8,128)} %bitcast.50), channel_id=1, source_target_pairs={{2,0},{4,2},{6,4},{8,6},{10,8},{12,10},{14,12},{16,14},{18,16},{20... | collective-permute-start | bytes 393224 | tf_op jit(solution)/shard_map/ppermute | solution.py:25
  57.7 7.8 %collective-permute-start.1 = (f32[2,128,128]{2,1,0:T(8,128)}, f32[2,128,128]{2,1,0:T(8,128)S(1)}, u32[]{:S(2)}, u32[]{:S(2)}) collective-permute-start(f32[2,128,128]{2,1,0:T(8,128)} %bitcast.49), channel_id=1, source_target_pairs={{766,0},{0,2},{2,4},{4,6},{6,8},{8,10},{10,12},{12,14},{14,16},{16... | collective-permute-start | bytes 393224 | tf_op jit(solution)/shard_map/ppermute | solution.py:25
Sparse Core Ops, SparseCore 0:
  10.4 26.3 all-gather.1
  64.5 382.0 all-reduce.2
where the time goes:
time: 457 us
  waiting for transfers between devices  391 us (86%)
  matrix products  18.3 us (4%)
  local copies, waits for them, and re-layouts  15.3 us (3%)
  between operations  14.2 us (3%)
  starting transfers between devices  13.9 us (3%)
    psum x1, waiting for transfers between devices, body(): lax.psum((self_part, neighbor_part), 'blk')  377 us
  transfers between devices with their start and end apart: 6, of which 4 were waited for; matrix products, arithmetic and copies ran while one was open for 4% of the time, Pallas kernels for 0%

commit v1 on v0

v1 whole, which is shorter than its diff:
```python
import functools

import jax
import jax.numpy as jnp
from jax import lax
from jax.experimental import pallas as pl
from jax.experimental.pallas import tpu as pltpu
from jax.sharding import PartitionSpec as P

HALO = 2
SIDE = 128
TORUS = (4, 12, 8)
CHUNKS = 4
BF16, F32 = jnp.bfloat16, jnp.float32


def dot(a, b):
    return jnp.dot(a, b, preferred_element_type=F32)


def kernel(
    torus,
    feat, grad, tiles, cols, self_w, neigh_w,
    fgrad, wgrad,
    tile_buf, feat_buf, grad_buf, w_buf, cols_v, index_v, index_s,
    chain, full_t, ext_hi, ext_lo, rim_out, rim_in, fg_buf,
    part, got_x, sum_x, got_y, sum_y, got_z, all_y, all_x, w_out,
    load_sem, tile_sem, out_sem, pair_send, pair_recv, rim_send, rim_recv,
    send_x, recv_x, send_y, recv_y, send_z, recv_z, send_ay, recv_ay, send_ax, recv_ax,
):
    nx, nz, ny = torus
    n = nx * nz * ny
    m, c = lax.axis_index("blk"), lax.axis_index("rep")
    x, z, y = m // (nz * ny), (m // ny) % nz, m % ny
    rows = grad.shape[0]
    blocks = rows // SIDE
    ext = blocks + 2 * HALO
    per = tiles.shape[0] // blocks
    rim = HALO * SIDE
    up, down = (m + 1) % n, (m + n - 1) % n
    other = 1 - c

    def at(xx, zz, yy):
        return (xx * nz + zz) * ny + yy

    group_x = [((x + k // 2) % nx, (c + k % 2) % 2) for k in range(1, 2 * nx)]
    group_y = [(y + k) % ny for k in range(1, ny)]
    group_z = [(z + k) % nz for k in range(1, nz)]
    group_ax = [(x + k) % nx for k in range(1, nx)]

    def remote(src, dst, send, recv, blk, rep):
        return pltpu.make_async_remote_copy(
            src_ref=src, dst_ref=dst, send_sem=send, recv_sem=recv,
            device_id={"blk": blk, "rep": rep}, device_id_type=pl.DeviceIdType.MESH,
        )

    own_cols = pl.ds(pl.multiple_of(c * SIDE, SIDE), SIDE)
    loads = [
        pltpu.make_async_copy(cols, cols_v, load_sem.at[0]),
        pltpu.make_async_copy(grad, grad_buf, load_sem.at[1]),
    ]
    chunk = tiles.shape[0] // CHUNKS
    tile_loads = [
        pltpu.make_async_copy(tiles.at[pl.ds(i * chunk, chunk)], tile_buf.at[pl.ds(i * chunk, chunk)], tile_sem.at[i])
        for i in range(CHUNKS)
    ]
    late_loads = [
        pltpu.make_async_copy(feat, feat_buf.at[pl.ds(rim, rows), own_cols], load_sem.at[2]),
        pltpu.make_async_copy(self_w, w_buf.at[0], load_sem.at[3]),
        pltpu.make_async_copy(neigh_w, w_buf.at[1], load_sem.at[4]),
    ]
    for copy in loads + tile_loads + late_loads:
        copy.start()

    barrier = pltpu.get_barrier_semaphore()
    peers = [(at(xx, z, y), cc) for xx, cc in group_x]
    peers += [(at(x, z, yy), c) for yy in group_y]
    peers += [(at(x, zz, y), c) for zz in group_z]
    peers += [(blk, rep) for blk in (up, down) for rep in (c, other)]
    for blk, rep in peers:
        pl.semaphore_signal(barrier, inc=1, device_id={"blk": blk, "rep": rep}, device_id_type=pl.DeviceIdType.MESH)

    loads[0].wait()
    count = tiles.shape[0]
    slot = cols_v[...] - m * blocks + HALO
    slot = jnp.where(slot < 0, slot + n * blocks, slot)
    slot = jnp.where(slot >= n * blocks, slot - n * blocks, slot)
    slot = jnp.concatenate([slot, jnp.full((1, SIDE - count), -1, jnp.int32)], axis=1)
    across = jnp.broadcast_to(slot, (SIDE, SIDE))
    along = across.T
    row = lax.broadcasted_iota(jnp.int32, (SIDE, SIDE), 0)
    lane = lax.broadcasted_iota(jnp.int32, (SIDE, SIDE), 1)
    before = jnp.max(jnp.where((across == along) & (row < lane), row, -1), axis=0, keepdims=True)
    final = jnp.max(jnp.where((along == lane) & (row < count), row, -1), axis=0, keepdims=True)
    index_v[0:1, :] = jnp.where(before < 0, count, before)
    index_v[1:2, :] = jnp.where(final < 0, count, final)
    to_scalar = pltpu.make_async_copy(index_v, index_s, load_sem.at[5])
    to_scalar.start()
    chain[count] = jnp.zeros((SIDE, SIDE), F32)
    to_scalar.wait()

    pl.semaphore_wait(barrier, len(peers))
    pair_feat = remote(feat, feat_buf.at[pl.ds(rim, rows), own_cols], pair_send.at[0], pair_recv.at[0], m, other)
    pair_feat.start()
    rims = []
    for k, rep in enumerate((c, other)):
        rims.append(remote(
            feat.at[pl.ds(0, rim)], feat_buf.at[pl.ds(rim + rows, rim), own_cols],
            rim_send.at[k], rim_recv.at[k], down, rep))
        rims.append(remote(
            feat.at[pl.ds(rows - rim, rim)], feat_buf.at[pl.ds(0, rim), own_cols],
            rim_send.at[2 + k], rim_recv.at[2 + k], up, rep))
    for copy in rims:
        copy.start()

    loads[1].wait()
    for i in range(CHUNKS):
        tile_loads[i].wait()

        def row_block(b, carry):
            span = pl.ds(pl.multiple_of(b * SIDE, SIDE), SIDE)
            g_t = grad_buf[span, :].T
            full_t[c, :, span] = g_t
            side = jnp.concatenate([tile_buf[b * per + k] for k in range(per)], axis=1)
            product = dot(g_t, side)
            for k in range(per):
                t = b * per + k
                chain[t] = chain[index_s[0, t]] + product[:, k * SIDE:(k + 1) * SIDE]
            return carry

        step = blocks // CHUNKS
        lax.fori_loop(i * step, (i + 1) * step, row_block, 0)

    pair_grad = remote(full_t.at[c], full_t.at[c], pair_send.at[1], pair_recv.at[1], m, other)
    pair_grad.start()
    for k in range(ext):
        span = pl.ds(k * SIDE, SIDE)
        value = chain[index_s[1, k]]
        hi = value.astype(BF16)
        ext_hi[:, span] = hi
        ext_lo[:, span] = (value - hi.astype(F32)).astype(BF16)
        if k < HALO:
            rim_out[0, k] = value
        elif k >= ext - HALO:
            rim_out[1, k - ext + HALO] = value
        elif 2 * HALO <= k < ext - 2 * HALO:
            full_t[2 + c, :, pl.ds((k - HALO) * SIDE, SIDE)] = hi
    sums = [
        remote(rim_out.at[0], rim_in.at[0], rim_send.at[4], rim_recv.at[4], down, c),
        remote(rim_out.at[1], rim_in.at[1], rim_send.at[5], rim_recv.at[5], up, c),
    ]
    for copy in sums:
        copy.start()

    late_loads[0].wait()
    pair_feat.wait_recv()
    share = SIDE // nx

    def put(which, value):
        for r in range(2):
            for q in range(nx):
                part[r, q, which * share:(which + 1) * share, :] = (
                    value[q * share:(q + 1) * share, r * SIDE:(r + 1) * SIDE])

    put(0, dot(full_t[c], feat_buf[rim:rim + rows, :]))
    for copy in rims:
        copy.wait_recv()
    every = feat_buf[...]
    put(1, dot(ext_hi[...], every) + dot(ext_lo[...], every))

    stage_x = []
    for xx, cc in group_x:
        stage_x.append(remote(
            part.at[cc, xx], got_x.at[2 * x + c], send_x.at[2 * xx + cc], recv_x.at[2 * x + c], at(xx, z, y), cc))
        stage_x[-1].start()

    for copy in sums:
        copy.wait_recv()
    for k in range(2 * HALO):
        low = k < HALO
        b = k if low else blocks - 2 * HALO + k
        span = pl.ds(b * SIDE, SIDE)
        value = chain[index_s[1, b + HALO]] + (rim_in[1, k] if low else rim_in[0, k - HALO])
        full_t[2 + c, :, span] = value.astype(BF16)
    pair_sum = remote(full_t.at[2 + c], full_t.at[2 + c], pair_send.at[2], pair_recv.at[2], m, other)
    pair_sum.start()

    got_x[2 * x + c] = part[c, x]
    for xx, cc in group_x:
        s = 2 * xx + cc
        pltpu.make_async_copy(part.at[c, x], got_x.at[s], recv_x.at[s]).wait()
    for cc in range(2):
        total = got_x[cc]
        for xx in range(1, nx):
            total = total + got_x[2 * xx + cc]
        sum_x[cc * 2 * share:(cc + 1) * 2 * share, :] = total

    piece = 4 * share // ny
    stage_y = []
    for yy in group_y:
        stage_y.append(remote(
            sum_x.at[pl.ds(pl.multiple_of(yy * piece, piece), piece)], got_y.at[y],
            send_y.at[yy], recv_y.at[y], at(x, z, yy), c))
        stage_y[-1].start()

    for copy in late_loads[1:]:
        copy.wait()
    pair_grad.wait_recv()
    pair_sum.wait_recv()
    weights = jnp.concatenate([w_buf[0], w_buf[1]], axis=1)
    wide = 2 * SIDE

    def feature_part(i, carry):
        span = pl.ds(pl.multiple_of(i * wide, wide), wide)
        fg_buf[span, :] = dot(weights, full_t[:, :, span].reshape(4 * SIDE, wide)).T
        return carry

    halves = rows // wide // 2
    lax.fori_loop(0, halves, feature_part, 0)
    outs = [
        pltpu.make_async_copy(
            fg_buf.at[pl.ds(i * (rows // 2), rows // 2)], fgrad.at[pl.ds(i * (rows // 2), rows // 2)], out_sem.at[i])
        for i in range(2)
    ]
    outs[0].start()

    got_y[y] = sum_x[pl.ds(pl.multiple_of(y * piece, piece), piece), :]
    for yy in group_y:
        pltpu.make_async_copy(sum_y, got_y.at[yy], recv_y.at[yy]).wait()
    total = got_y[0]
    for yy in range(1, ny):
        total = total + got_y[yy]
    sum_y[...] = total

    stage_z = []
    for zz in group_z:
        stage_z.append(remote(sum_y, got_z.at[z], send_z.at[zz], recv_z.at[z], at(x, zz, y), c))
        stage_z[-1].start()
    lax.fori_loop(halves, 2 * halves, feature_part, 0)
    outs[1].start()

    got_z[z] = total
    for zz in group_z:
        pltpu.make_async_copy(sum_y, got_z.at[zz], recv_z.at[zz]).wait()
    total = got_z[0]
    for zz in range(1, nz):
        total = total + got_z[zz]
    own_piece = pl.ds(pl.multiple_of(y * piece, piece), piece)
    all_y[own_piece, :] = total

    back_y = []
    for yy in group_y:
        back_y.append(remote(all_y.at[own_piece], all_y.at[own_piece], send_ay.at[yy], recv_ay.at[y], at(x, z, yy), c))
        back_y[-1].start()
    for yy in group_y:
        other_piece = pl.ds(pl.multiple_of(yy * piece, piece), piece)
        pltpu.make_async_copy(all_y.at[own_piece], all_y.at[other_piece], recv_ay.at[yy]).wait()
    back_x = []
    for xx in group_ax:
        back_x.append(remote(all_y, all_x.at[x], send_ax.at[xx], recv_ax.at[x], at(xx, z, y), c))
        back_x[-1].start()
    all_x[x] = all_y[...]
    for xx in group_ax:
        pltpu.make_async_copy(all_y, all_x.at[xx], recv_ax.at[xx]).wait()
    for which in range(2):
        for cc in range(2):
            base = (2 * cc + which) * share
            value = jnp.concatenate([all_x[q, base:base + share, :] for q in range(nx)], axis=0)
            w_out[which, :, cc * SIDE:(cc + 1) * SIDE] = value.T
    last = pltpu.make_async_copy(w_out, wgrad, out_sem.at[2])
    last.start()

    for copy in [pair_feat, pair_grad, pair_sum] + rims + sums + stage_x + stage_y + stage_z + back_y + back_x:
        copy.wait_send()
    for copy in outs:
        copy.wait()
    last.wait()


def body(torus, features, out_grad, block_tiles, block_cols, self_weight, neighbor_weight):
    nx, nz, ny = torus
    rows, columns = features.shape
    width = self_weight.shape[1]
    count = block_tiles.shape[0]
    blocks = rows // SIDE
    ext = blocks + 2 * HALO
    share = SIDE // nx
    piece = 4 * share // ny
    dma = pltpu.SemaphoreType.DMA
    anywhere = pl.BlockSpec(memory_space=pl.ANY)
    feature_grad, weight_grad = pl.pallas_call(
        functools.partial(kernel, torus),
        out_shape=(
            jax.ShapeDtypeStruct((rows, columns), F32),
            jax.ShapeDtypeStruct((2, columns, width), F32),
        ),
        in_specs=[anywhere] * 6,
        out_specs=(anywhere, anywhere),
        scratch_shapes=[
            pltpu.VMEM((count, SIDE, SIDE), BF16),
            pltpu.VMEM((ext * SIDE, 2 * SIDE), BF16),
            pltpu.VMEM((rows, columns), BF16),
            pltpu.VMEM((2, SIDE, width), BF16),
            pltpu.VMEM((1, count), jnp.int32),
            pltpu.VMEM((8, SIDE), jnp.int32),
            pltpu.SMEM((8, SIDE), jnp.int32),
            pltpu.VMEM((count + 1, SIDE, SIDE), F32),
            pltpu.VMEM((4, SIDE, rows), BF16),
            pltpu.VMEM((SIDE, ext * SIDE), BF16),
            pltpu.VMEM((SIDE, ext * SIDE), BF16),
            pltpu.VMEM((2, HALO, SIDE, SIDE), F32),
            pltpu.VMEM((2, HALO, SIDE, SIDE), F32),
            pltpu.VMEM((rows, columns), F32),
            pltpu.VMEM((2, nx, 2 * share, SIDE), F32),
            pltpu.VMEM((2 * nx, 2 * share, SIDE), F32),
            pltpu.VMEM((4 * share, SIDE), F32),
            pltpu.VMEM((ny, piece, SIDE), F32),
            pltpu.VMEM((piece, SIDE), F32),
            pltpu.VMEM((nz, piece, SIDE), F32),
            pltpu.VMEM((4 * share, SIDE), F32),
            pltpu.VMEM((nx, 4 * share, SIDE), F32),
            pltpu.VMEM((2, columns, width), F32),
            dma((6,)), dma((CHUNKS,)), dma((3,)), dma((3,)), dma((3,)), dma((6,)), dma((6,)),
            dma((2 * nx,)), dma((2 * nx,)), dma((ny,)), dma((ny,)), dma((nz,)), dma((nz,)),
            dma((ny,)), dma((ny,)), dma((nx,)), dma((nx,)),
        ],
        compiler_params=pltpu.CompilerParams(
            collective_id=0, has_side_effects=True, vmem_limit_bytes=40 * 1024 * 1024
        ),
        cost_estimate=pl.CostEstimate(flops=1100000000, bytes_accessed=4500000, transcendentals=0),
    )(features, out_grad, block_tiles, block_cols.reshape(1, count), self_weight, neighbor_weight)
    return feature_grad, weight_grad[0], weight_grad[1]


def solution(mesh):
    in_specs = (
        P("blk", "rep"),
        P("blk", "rep"),
        P("blk", None, None),
        P("blk"),
        P("rep", None),
        P("rep", None),
    )
    out_specs = (P("blk", "rep"), P("rep", None), P("rep", None))
    step = functools.partial(body, TORUS)
    return jax.shard_map(step, mesh=mesh, in_specs=in_specs, out_specs=out_specs, check_vma=False)
```

time: 457 us -> 61.4 us (0.13)
  the two profiles are of different devices: /device:TPU:26 before, /device:TPU:4 now
where the time goes in v1:
time: 61.4 us; the launch traced here: 61.1 us
  Pallas kernels  52.7 us (86%)
  local copies, waits for them, and re-layouts  7.68 us (13%)
  between operations  0.65 us (1%)
    pallas_call x1, Pallas kernels, body(): pl.pallas_call(functools.partial(kernel, torus), out_shape=(jax.ShapeDtyp...  52.7 us
    unnamed x13, local copies, waits for them, and re-layouts  6.97 us

profile of v1, /device:TPU:4, one launch (start us, length us, event | category | flops | bytes accessed | tf_op | source)
XLA Modules:
  0.0 61.1 jit_solution(14554990928427718862)
XLA Ops:
  0.6 0.0 copy-start
  0.6 1.6 %copy-done = bf16[64,128,128]{2,1,0:T(8,128)(2,1)S(1)} copy-done((bf16[64,128,128]{2,1,0:T(8,128)(2,1)S(1)}, bf16[64,128,128]{2,1,0:T(8,128)(2,1)}, u32[]{:S(2)}) %copy-start) | copy-done | bytes 2097176
  2.2 0.0 copy-start.1
  2.2 1.0 %copy-done.1 = bf16[2048,128]{1,0:T(8,128)(2,1)S(1)} copy-done((bf16[2048,128]{1,0:T(8,128)(2,1)S(1)}, bf16[2048,128]{1,0:T(8,128)(2,1)}, u32[]{:S(2)}) %copy-start.1) | copy-done | bytes 524312
  3.3 0.0 copy-start.2
  3.3 1.0 %copy-done.2 = bf16[2048,128]{1,0:T(8,128)(2,1)S(1)} copy-done((bf16[2048,128]{1,0:T(8,128)(2,1)S(1)}, bf16[2048,128]{1,0:T(8,128)(2,1)}, u32[]{:S(2)}) %copy-start.2) | copy-done | bytes 524312
  4.3 0.0 copy-start.3
  4.3 0.8 %copy-done.3 = bf16[128,256]{1,0:T(8,128)(2,1)S(1)} copy-done((bf16[128,256]{1,0:T(8,128)(2,1)S(1)}, bf16[128,256]{1,0:T(8,128)(2,1)}, u32[]{:S(2)}) %copy-start.3) | copy-done | bytes 65560
  5.1 0.0 copy-start.4
  5.2 0.8 %copy-done.4 = bf16[128,256]{1,0:T(8,128)(2,1)S(1)} copy-done((bf16[128,256]{1,0:T(8,128)(2,1)S(1)}, bf16[128,256]{1,0:T(8,128)(2,1)}, u32[]{:S(2)}) %copy-start.4) | copy-done | bytes 65560
  6.0 0.0 copy-start.5
  6.0 0.7 %copy-done.5 = s32[64]{0:T(128)S(1)} copy-done((s32[64]{0:T(128)S(1)}, s32[64]{0:T(128)}, u32[]{:S(2)}) %copy-start.5) | copy-done | bytes 280
  6.6 52.7 %shard_map.85 = (f32[2048,128]{1,0:T(8,128)S(1)}, f32[2,128,256]{2,1,0:T(8,128)S(1)}) custom-call(bf16[2048,128]{1,0:T(8,128)(2,1)S(1)} %copy-done.1, bf16[2048,128]{1,0:T(8,128)(2,1)S(1)} %copy-done.2, bf16[64,128,128]{2,1,0:T(8,128)(2,1)S(1)} %copy-done, s32[1,64]{1,0:T(1,128)S(1)} %bitcast.5, bf16[128,256]{1,0:T(8,128)(2,1)S(1)} %copy-done.3, ...), custom_call_target="tpu_custom_call" | custom-call | flops 1100000000 | bytes 4500000 | tf_op jit(solution)/shard_map/pallas_call | solution.py:291
  59.4 0.7 %slice_bitcast_fusion = (f32[128,256]{1,0:T(8,128)}, f32[128,256]{1,0:T(8,128)}) fusion(f32[2,128,256]{2,1,0:T(8,128)S(1)} %get-tuple-element.6), kind=kLoop, calls=%fused_computation | loop fusion | bytes 524288 | tf_op jit(solution)/shard_map/squeeze | solution.py:332
  60.1 1.0 %copy.10 = f32[2048,128]{1,0:T(8,128)} copy(f32[2048,128]{1,0:T(8,128)S(1)} %get-tuple-element.12) | data formatting | bytes 2097152
Async XLA Ops:
  0.6 1.6 %copy-start = (bf16[64,128,128]{2,1,0:T(8,128)(2,1)S(1)}, bf16[64,128,128]{2,1,0:T(8,128)(2,1)}, u32[]{:S(2)}) copy-start(bf16[64,128,128]{2,1,0:T(8,128)(2,1)} %tiles.1) | copy-start | bytes 6291460
  2.2 1.0 %copy-start.1 = (bf16[2048,128]{1,0:T(8,128)(2,1)S(1)}, bf16[2048,128]{1,0:T(8,128)(2,1)}, u32[]{:S(2)}) copy-start(bf16[2048,128]{1,0:T(8,128)(2,1)} %feat.1) | copy-start | bytes 1572868
  3.3 1.0 %copy-start.2 = (bf16[2048,128]{1,0:T(8,128)(2,1)S(1)}, bf16[2048,128]{1,0:T(8,128)(2,1)}, u32[]{:S(2)}) copy-start(bf16[2048,128]{1,0:T(8,128)(2,1)} %grad.1) | copy-start | bytes 1572868
  4.3 0.8 %copy-start.3 = (bf16[128,256]{1,0:T(8,128)(2,1)S(1)}, bf16[128,256]{1,0:T(8,128)(2,1)}, u32[]{:S(2)}) copy-start(bf16[128,256]{1,0:T(8,128)(2,1)} %self_w.1) | copy-start | bytes 196612
  5.1 0.8 %copy-start.4 = (bf16[128,256]{1,0:T(8,128)(2,1)S(1)}, bf16[128,256]{1,0:T(8,128)(2,1)}, u32[]{:S(2)}) copy-start(bf16[128,256]{1,0:T(8,128)(2,1)} %neigh_w.1) | copy-start | bytes 196612
  6.0 0.7 %copy-start.5 = (s32[64]{0:T(128)S(1)}, s32[64]{0:T(128)}, u32[]{:S(2)}) copy-start(s32[64]{0:T(128)} %param.9) | copy-start | bytes 772

commit v2 on v1

v2 whole, which is shorter than its diff:
```python
import functools

import jax
import jax.numpy as jnp
from jax import lax
from jax.experimental import pallas as pl
from jax.experimental.pallas import tpu as pltpu
from jax.sharding import PartitionSpec as P

HALO = 2
SIDE = 128
TORUS = (4, 12, 8)
CHUNKS = 4
VMEM_BYTES = 60 * 1024 * 1024
BF16, F32 = jnp.bfloat16, jnp.float32


def dot(a, b):
    return jnp.dot(a, b, preferred_element_type=F32)


def kernel(
    torus,
    feat, grad, tiles, cols, self_w, neigh_w,
    fgrad, wgrad,
    tile_buf, feat_buf, grad_buf, w_buf, cols_v, index_v, index_s,
    chain, full_t, low_t, rim_out, rim_in,
    part, got_x, sum_x, got_y, sum_y, got_z, every,
    load_sem, tile_sem, pair_send, pair_recv, rim_send, rim_recv,
    send_x, recv_x, send_y, recv_y, send_z, recv_z, send_ay, recv_ay, send_ax, recv_ax,
):
    nx, nz, ny = torus
    n = nx * nz * ny
    m, c = lax.axis_index("blk"), lax.axis_index("rep")
    x, z, y = m // (nz * ny), (m // ny) % nz, m % ny
    rows = grad.shape[0]
    blocks = rows // SIDE
    count = tiles.shape[0]
    per = count // blocks
    up, down = (m + 1) % n, (m + n - 1) % n
    other = 1 - c

    def at(xx, zz, yy):
        return (xx * nz + zz) * ny + yy

    def far_first(size):
        return sorted(range(1, size), key=lambda k: -min(k, size - k))

    group_x = [((x + k) % nx, (c + j) % 2) for k in far_first(nx) + [0] for j in ((0, 1) if k else (1,))]
    group_y = [(y + k) % ny for k in far_first(ny)]
    group_z = [(z + k) % nz for k in far_first(nz)]
    group_ax = [(x + k) % nx for k in far_first(nx)]

    def remote(src, dst, send, recv, blk, rep):
        return pltpu.make_async_remote_copy(
            src_ref=src, dst_ref=dst, send_sem=send, recv_sem=recv,
            device_id={"blk": blk, "rep": rep}, device_id_type=pl.DeviceIdType.MESH,
        )

    def arrived(like, recv):
        pltpu.make_async_copy(like, like, recv).wait()

    barrier = pltpu.get_barrier_semaphore()
    peers = [(at(x, zz, y), c) for zz in group_z]
    peers += [(at(x, z, yy), c) for yy in group_y]
    peers += [(at(xx, z, y), cc) for xx, cc in group_x]
    peers += [(up, c), (down, c)]
    for blk, rep in peers:
        pl.semaphore_signal(barrier, inc=1, device_id={"blk": blk, "rep": rep}, device_id_type=pl.DeviceIdType.MESH)

    own_cols = pl.ds(pl.multiple_of(c * SIDE, SIDE), SIDE)
    first_loads = [
        pltpu.make_async_copy(cols, cols_v, load_sem.at[0]),
        pltpu.make_async_copy(grad, grad_buf, load_sem.at[1]),
    ]
    chunk = count // CHUNKS
    order = [0, CHUNKS - 1] + list(range(1, CHUNKS - 1))
    tile_loads = {
        i: pltpu.make_async_copy(tiles.at[pl.ds(i * chunk, chunk)], tile_buf.at[pl.ds(i * chunk, chunk)], tile_sem.at[i])
        for i in order
    }
    late_loads = [
        pltpu.make_async_copy(feat, feat_buf.at[:, own_cols], load_sem.at[2]),
        pltpu.make_async_copy(self_w, w_buf.at[0], load_sem.at[3]),
        pltpu.make_async_copy(neigh_w, w_buf.at[1], load_sem.at[4]),
    ]
    for copy in first_loads + [tile_loads[i] for i in order] + late_loads:
        copy.start()

    ahead = {0: 0, CHUNKS - 1: (2 - CHUNKS) * chunk} | {i: chunk for i in range(1, CHUNKS - 1)}

    def place(t):
        return jnp.where(t < chunk, t, jnp.where(t >= count - chunk, t + ahead[CHUNKS - 1], t + chunk))

    first_loads[0].wait()
    slot = cols_v[...] - m * blocks
    slot = jnp.concatenate([slot, jnp.full((1, SIDE - count), -1, jnp.int32)], axis=1)
    across = jnp.broadcast_to(slot, (SIDE, SIDE))
    along = across.T
    row = lax.broadcasted_iota(jnp.int32, (SIDE, SIDE), 0)
    lane = lax.broadcasted_iota(jnp.int32, (SIDE, SIDE), 1)
    row_at, lane_at = place(row), place(lane)
    before = jnp.max(jnp.where((across == along) & (row_at < lane_at), row_at, -1), axis=0, keepdims=True)
    final = jnp.max(jnp.where((along == lane) & (row < count), row_at, -1), axis=0, keepdims=True)
    index_v[0:1, :] = jnp.where(before < 0, count, before)
    index_v[1:2, :] = jnp.where(final < 0, count, final)
    to_scalar = pltpu.make_async_copy(index_v, index_s, load_sem.at[5])
    to_scalar.start()
    chain[count] = jnp.zeros((SIDE, SIDE), F32)
    to_scalar.wait()

    def row_block(shift, b, carry):
        span = pl.ds(pl.multiple_of(b * SIDE, SIDE), SIDE)
        g_t = grad_buf[span, :].T
        full_t[c, :, span] = g_t
        product = dot(g_t, jnp.concatenate([tile_buf[b * per + k] for k in range(per)], axis=1))
        for k in range(per):
            t = b * per + k
            chain[t + shift] = chain[index_s[0, t]] + product[:, k * SIDE:(k + 1) * SIDE]
        return carry

    def tile_work(i):
        tile_loads[i].wait()
        step = blocks // CHUNKS
        lax.fori_loop(i * step, (i + 1) * step, functools.partial(row_block, ahead[i]), 0)

    first_loads[1].wait()
    for i in order[:2]:
        tile_work(i)
    for k in range(HALO):
        rim_out[0, k] = chain[k * per].astype(BF16)
        rim_out[1, k] = chain[(blocks - HALO + k) * per + ahead[CHUNKS - 1]].astype(BF16)

    pl.semaphore_wait(barrier, len(peers))
    sums = [
        remote(rim_out.at[0], rim_in.at[0], rim_send.at[0], rim_recv.at[0], down, c),
        remote(rim_out.at[1], rim_in.at[1], rim_send.at[1], rim_recv.at[1], up, c),
    ]
    for copy in sums:
        copy.start()
    pair_feat = remote(feat, feat_buf.at[:, own_cols], pair_send.at[0], pair_recv.at[0], m, other)
    pair_feat.start()
    for i in order[2:]:
        tile_work(i)

    def column_block(b, value):
        span = pl.ds(b * SIDE, SIDE)
        hi = value.astype(BF16)
        full_t[2 + c, :, span] = hi
        low_t[:, span] = (value - hi.astype(F32)).astype(BF16)

    for b in range(HALO, blocks - HALO):
        column_block(b, chain[index_s[1, b]])

    share = SIDE // nx
    stage_x = [[], []]

    def send_share(which, value):
        for r in range(2):
            for q in range(nx):
                part[which, r, q] = value[q * share:(q + 1) * share, r * SIDE:(r + 1) * SIDE]
        for xx, cc in group_x:
            stage_x[which].append(remote(
                part.at[which, cc, xx], got_x.at[which, 2 * x + c],
                send_x.at[which, 2 * xx + cc], recv_x.at[which, 2 * x + c], at(xx, z, y), cc))
            stage_x[which][-1].start()
        got_x[which, 2 * x + c] = part[which, c, x]

    late_loads[0].wait()
    pair_feat.wait_recv()
    send_share(0, dot(full_t[c], feat_buf[...]))
    for copy in sums:
        copy.wait_recv()
    for k in range(HALO):
        b = blocks - 1 - k
        column_block(b, chain[index_s[1, b]] + rim_in[0, k].astype(F32))
        b = HALO - 1 - k
        column_block(b, chain[index_s[1, b]] + rim_in[1, k].astype(F32))
    send_share(1, dot(full_t[2 + c], feat_buf[...]) + dot(low_t[...], feat_buf[...]))
    pair_grad = remote(full_t.at[c], full_t.at[c], pair_send.at[1], pair_recv.at[1], m, other)
    pair_grad.start()
    pair_sum = remote(full_t.at[2 + c], full_t.at[2 + c], pair_send.at[2], pair_recv.at[2], m, other)
    pair_sum.start()
    for copy in late_loads[1:]:
        copy.wait()

    for which in range(2):
        for xx, cc in group_x:
            arrived(part.at[which, c, x], recv_x.at[which, 2 * xx + cc])
        for cc in range(2):
            total = got_x[which, cc]
            for xx in range(1, nx):
                total = total + got_x[which, 2 * xx + cc]
            sum_x[(2 * cc + which) * share:(2 * cc + which + 1) * share, :] = total

    piece = 4 * share // ny
    own_piece = pl.ds(pl.multiple_of(y * piece, piece), piece)
    stage_y = []
    for yy in group_y:
        stage_y.append(remote(
            sum_x.at[pl.ds(pl.multiple_of(yy * piece, piece), piece)], got_y.at[y],
            send_y.at[yy], recv_y.at[y], at(x, z, yy), c))
        stage_y[-1].start()
    got_y[y] = sum_x[own_piece, :]

    pair_grad.wait_recv()
    pair_sum.wait_recv()
    weights = jnp.concatenate([w_buf[0], w_buf[1]], axis=1)
    wide = 2 * SIDE

    def feature_part(i, carry):
        span = pl.ds(pl.multiple_of(i * wide, wide), wide)
        fgrad[span, :] = dot(weights, full_t[:, :, span].reshape(4 * SIDE, wide)).T
        return carry

    halves = rows // wide // 2
    lax.fori_loop(0, halves, feature_part, 0)

    for yy in group_y:
        arrived(sum_y, recv_y.at[yy])
    total = got_y[0]
    for yy in range(1, ny):
        total = total + got_y[yy]
    sum_y[...] = total

    stage_z = []
    for zz in group_z:
        stage_z.append(remote(sum_y, got_z.at[z], send_z.at[zz], recv_z.at[z], at(x, zz, y), c))
        stage_z[-1].start()
    got_z[z] = total
    lax.fori_loop(halves, 2 * halves, feature_part, 0)
    for zz in group_z:
        arrived(sum_y, recv_z.at[zz])
    total = got_z[0]
    for zz in range(1, nz):
        total = total + got_z[zz]
    every[x, own_piece, :] = total

    back = []
    for yy in group_y:
        back.append(remote(
            every.at[x, own_piece], every.at[x, own_piece], send_ay.at[yy], recv_ay.at[y], at(x, z, yy), c))
        back[-1].start()
    for yy in [y] + group_y[::-1]:
        rows_of = pl.ds(pl.multiple_of(yy * piece, piece), piece)
        if yy is not y:
            arrived(every.at[x, rows_of], recv_ay.at[yy])
        for xx in group_ax:
            back.append(remote(
                every.at[x, rows_of], every.at[x, rows_of], send_ax.at[xx, yy], recv_ax.at[x, yy], at(xx, z, y), c))
            back[-1].start()
    for yy in [y] + group_y[::-1]:
        rows_of = pl.ds(pl.multiple_of(yy * piece, piece), piece)
        for xx in group_ax:
            arrived(every.at[xx, rows_of], recv_ax.at[xx, yy])
    for which in range(2):
        for cc in range(2):
            base = (2 * cc + which) * share
            value = jnp.concatenate([every[q, base:base + share, :] for q in range(nx)], axis=0)
            wgrad[which, :, cc * SIDE:(cc + 1) * SIDE] = value.T

    for copy in [pair_feat, pair_grad, pair_sum] + sums + stage_x[0] + stage_x[1] + stage_y + stage_z + back:
        copy.wait_send()


def body(torus, features, out_grad, block_tiles, block_cols, self_weight, neighbor_weight):
    nx, nz, ny = torus
    rows, columns = features.shape
    width = self_weight.shape[1]
    count = block_tiles.shape[0]
    share = SIDE // nx
    piece = 4 * share // ny
    dma = pltpu.SemaphoreType.DMA
    feature_grad, weight_grad = pl.pallas_call(
        functools.partial(kernel, torus),
        out_shape=(pltpu.VMEM((rows, columns), F32), pltpu.VMEM((2, columns, width), F32)),
        in_specs=[pl.BlockSpec(memory_space=pl.ANY)] * 6,
        out_specs=(pl.BlockSpec(memory_space=pltpu.VMEM),) * 2,
        scratch_shapes=[
            pltpu.VMEM((count, SIDE, SIDE), BF16),
            pltpu.VMEM((rows, 2 * SIDE), BF16),
            pltpu.VMEM((rows, columns), BF16),
            pltpu.VMEM((2, SIDE, width), BF16),
            pltpu.VMEM((1, count), jnp.int32),
            pltpu.VMEM((8, SIDE), jnp.int32),
            pltpu.SMEM((8, SIDE), jnp.int32),
            pltpu.VMEM((count + 1, SIDE, SIDE), F32),
            pltpu.VMEM((4, SIDE, rows), BF16),
            pltpu.VMEM((SIDE, rows), BF16),
            pltpu.VMEM((2, HALO, SIDE, SIDE), BF16),
            pltpu.VMEM((2, HALO, SIDE, SIDE), BF16),
            pltpu.VMEM((2, 2, nx, share, SIDE), F32),
            pltpu.VMEM((2, 2 * nx, share, SIDE), F32),
            pltpu.VMEM((4 * share, SIDE), F32),
            pltpu.VMEM((ny, piece, SIDE), F32),
            pltpu.VMEM((piece, SIDE), F32),
            pltpu.VMEM((nz, piece, SIDE), F32),
            pltpu.VMEM((nx, 4 * share, SIDE), F32),
            dma((6,)), dma((CHUNKS,)), dma((3,)), dma((3,)), dma((2,)), dma((2,)),
            dma((2, 2 * nx)), dma((2, 2 * nx)), dma((ny,)), dma((ny,)), dma((nz,)), dma((nz,)),
            dma((ny,)), dma((ny,)), dma((nx, ny)), dma((nx, ny)),
        ],
        compiler_params=pltpu.CompilerParams(
            collective_id=0, has_side_effects=True, vmem_limit_bytes=VMEM_BYTES
        ),
        cost_estimate=pl.CostEstimate(flops=1100000000, bytes_accessed=4500000, transcendentals=0),
    )(features, out_grad, block_tiles, block_cols.reshape(1, count), self_weight, neighbor_weight)
    return feature_grad, weight_grad[0], weight_grad[1]


def solution(mesh):
    in_specs = (
        P("blk", "rep"),
        P("blk", "rep"),
        P("blk", None, None),
        P("blk"),
        P("rep", None),
        P("rep", None),
    )
    out_specs = (P("blk", "rep"), P("rep", None), P("rep", None))
    step = functools.partial(body, TORUS)
    return jax.shard_map(step, mesh=mesh, in_specs=in_specs, out_specs=out_specs, check_vma=False)
```

time: 61.4 us -> 50 us (0.81)
  the two profiles are of different devices: /device:TPU:4 before, /device:TPU:8 now
where the time goes in v2:
time: 50 us; the launch traced here: 49.9 us
  Pallas kernels  47.5 us (95%)
  local copies, waits for them, and re-layouts  1.69 us (3%)
  between operations  0.64 us (1%)
    pallas_call x1, Pallas kernels, body(): pl.pallas_call(functools.partial(kernel, torus), out_shape=(pltpu.VMEM((r...  47.5 us

profile of v2, /device:TPU:8, one launch (start us, length us, event | category | flops | bytes accessed | tf_op | source)
XLA Modules:
  0.0 49.9 jit_solution(2424802958774839093)
XLA Ops:
  0.6 47.5 %shard_map.85 = (f32[2048,128]{1,0:T(8,128)S(1)}, f32[2,128,256]{2,1,0:T(8,128)S(1)}) custom-call(bf16[2048,128]{1,0:T(8,128)(2,1)} %feat.1, bf16[2048,128]{1,0:T(8,128)(2,1)} %grad.1, bf16[64,128,128]{2,1,0:T(8,128)(2,1)} %tiles.1, s32[1,64]{1,0:T(1,128)} %bitcast.5, bf16[128,256]{1,0:T(8,128)(2,1)} %self_w.1, bf16[128,256]{1,0:T(8,128)(2,1)} %neigh_w.1), custom_call_target="tpu_custom_call" | custom-call | flops 1100000000 | bytes 4500000 | tf_op jit(solution)/shard_map/pallas_call | solution.py:274
  48.2 1.0 %copy.10 = f32[2048,128]{1,0:T(8,128)} copy(f32[2048,128]{1,0:T(8,128)S(1)} %get-tuple-element.9) | data formatting | bytes 2097152
  49.2 0.7 %slice_bitcast_fusion = (f32[128,256]{1,0:T(8,128)}, f32[128,256]{1,0:T(8,128)}) fusion(f32[2,128,256]{2,1,0:T(8,128)S(1)} %get-tuple-element.6), kind=kLoop, calls=%fused_computation | loop fusion | bytes 524288 | tf_op jit(solution)/shard_map/squeeze | solution.py:308

commit v3 on v2

--- a/solution.py
+++ b/solution.py
@@ -24,10 +24,10 @@
     feat, grad, tiles, cols, self_w, neigh_w,
     fgrad, wgrad,
     tile_buf, feat_buf, grad_buf, w_buf, cols_v, index_v, index_s,
-    chain, full_t, low_t, rim_out, rim_in,
+    chain, full_t, low_t, rim_tiles, rim_out, rim_in,
     part, got_x, sum_x, got_y, sum_y, got_z, every,
     load_sem, tile_sem, pair_send, pair_recv, rim_send, rim_recv,
-    send_x, recv_x, send_y, recv_y, send_z, recv_z, send_ay, recv_ay, send_ax, recv_ax,
+    heard_1, heard_2, heard_3, send_x, recv_x, send_y, recv_y, send_z, recv_z, send_ay, recv_ay, send_ax, recv_ax,
 ):
     nx, nz, ny = torus
     n = nx * nz * ny
@@ -60,78 +60,71 @@
     def arrived(like, recv):
         pltpu.make_async_copy(like, like, recv).wait()
 
+    def signal(sem, blk, rep):
+        pl.semaphore_signal(sem, inc=1, device_id={"blk": blk, "rep": rep}, device_id_type=pl.DeviceIdType.MESH)
+
     barrier = pltpu.get_barrier_semaphore()
-    peers = [(at(x, zz, y), c) for zz in group_z]
-    peers += [(at(x, z, yy), c) for yy in group_y]
-    peers += [(at(xx, z, y), cc) for xx, cc in group_x]
-    peers += [(up, c), (down, c)]
-    for blk, rep in peers:
-        pl.semaphore_signal(barrier, inc=1, device_id={"blk": blk, "rep": rep}, device_id_type=pl.DeviceIdType.MESH)
+    near = [(at(x, (z + k) % nz, y), c) for k in (1, nz - 1)] + [(at(x, z, (y + k) % ny), c) for k in (1, ny - 1)]
+    near += [(at((x + k) % nx, z, y), cc) for k in (1, nx - 1) for cc in (c, other)] + [(m, other), (up, c), (down, c)]
+    for blk, rep in near:
+        signal(barrier, blk, rep)
+
+    def pass_on(sems, step, axes):
+        for k in (step, -step):
+            to = {"x": at((x + k + nx) % nx, z, y), "y": at(x, z, (y + k + ny) % ny), "z": at(x, (z + k + nz) % nz, y)}
+            for i, axis in enumerate(axes):
+                signal(sems.at[i], to[axis], c)
+
+    def hear(sems, axes):
+        for i in range(len(axes)):
+            pl.semaphore_wait(sems.at[i], 2)
 
     own_cols = pl.ds(pl.multiple_of(c * SIDE, SIDE), SIDE)
-    first_loads = [
-        pltpu.make_async_copy(cols, cols_v, load_sem.at[0]),
-        pltpu.make_async_copy(grad, grad_buf, load_sem.at[1]),
+    rim = HALO * SIDE
+    ends = [k for k in range(HALO)] + [blocks - HALO + k for k in range(HALO)]
+    rim_loads = [
+        pltpu.make_async_copy(grad.at[pl.ds(0, rim)], grad_buf.at[pl.ds(0, rim)], load_sem.at[0]),
+        pltpu.make_async_copy(grad.at[pl.ds(rows - rim, rim)], grad_buf.at[pl.ds(rows - rim, rim)], load_sem.at[1]),
     ]
+    for k, b in enumerate(ends):
+        rim_loads.append(pltpu.make_async_copy(tiles.at[b * per], rim_tiles.at[k], load_sem.at[2 + k]))
+    load_cols = pltpu.make_async_copy(cols, cols_v, load_sem.at[6])
+    load_grad = pltpu.make_async_copy(
+        grad.at[pl.ds(rim, rows - 2 * rim)], grad_buf.at[pl.ds(rim, rows - 2 * rim)], load_sem.at[7])
     chunk = count // CHUNKS
-    order = [0, CHUNKS - 1] + list(range(1, CHUNKS - 1))
-    tile_loads = {
-        i: pltpu.make_async_copy(tiles.at[pl.ds(i * chunk, chunk)], tile_buf.at[pl.ds(i * chunk, chunk)], tile_sem.at[i])
-        for i in order
-    }
+    tile_loads = [
+        pltpu.make_async_copy(tiles.at[pl.ds(i * chunk, chunk)], tile_buf.at[pl.ds(i * chunk, chunk)], tile_sem.at[i])
+        for i in range(CHUNKS)
+    ]
     late_loads = [
-        pltpu.make_async_copy(feat, feat_buf.at[:, own_cols], load_sem.at[2]),
-        pltpu.make_async_copy(self_w, w_buf.at[0], load_sem.at[3]),
-        pltpu.make_async_copy(neigh_w, w_buf.at[1], load_sem.at[4]),
+        pltpu.make_async_copy(feat, feat_buf.at[:, own_cols], load_sem.at[8]),
+        pltpu.make_async_copy(self_w, w_buf.at[0], load_sem.at[9]),
+        pltpu.make_async_copy(neigh_w, w_buf.at[1], load_sem.at[10]),
     ]
-    for copy in first_loads + [tile_loads[i] for i in order] + late_loads:
+    for copy in [load_cols] + rim_loads + [load_grad] + tile_loads + late_loads:
         copy.start()
 
-    ahead = {0: 0, CHUNKS - 1: (2 - CHUNKS) * chunk} | {i: chunk for i in range(1, CHUNKS - 1)}
-
-    def place(t):
-        return jnp.where(t < chunk, t, jnp.where(t >= count - chunk, t + ahead[CHUNKS - 1], t + chunk))
-
-    first_loads[0].wait()
+    load_cols.wait()
     slot = cols_v[...] - m * blocks
     slot = jnp.concatenate([slot, jnp.full((1, SIDE - count), -1, jnp.int32)], axis=1)
     across = jnp.broadcast_to(slot, (SIDE, SIDE))
     along = across.T
     row = lax.broadcasted_iota(jnp.int32, (SIDE, SIDE), 0)
     lane = lax.broadcasted_iota(jnp.int32, (SIDE, SIDE), 1)
-    row_at, lane_at = place(row), place(lane)
-    before = jnp.max(jnp.where((across == along) & (row_at < lane_at), row_at, -1), axis=0, keepdims=True)
-    final = jnp.max(jnp.where((along == lane) & (row < count), row_at, -1), axis=0, keepdims=True)
+    before = jnp.max(jnp.where((across == along) & (row < lane), row, -1), axis=0, keepdims=True)
+    final = jnp.max(jnp.where((along == lane) & (row < count), row, -1), axis=0, keepdims=True)
     index_v[0:1, :] = jnp.where(before < 0, count, before)
     index_v[1:2, :] = jnp.where(final < 0, count, final)
-    to_scalar = pltpu.make_async_copy(index_v, index_s, load_sem.at[5])
+    to_scalar = pltpu.make_async_copy(index_v, index_s, load_sem.at[11])
     to_scalar.start()
     chain[count] = jnp.zeros((SIDE, SIDE), F32)
-    to_scalar.wait()
-
-    def row_block(shift, b, carry):
-        span = pl.ds(pl.multiple_of(b * SIDE, SIDE), SIDE)
-        g_t = grad_buf[span, :].T
-        full_t[c, :, span] = g_t
-        product = dot(g_t, jnp.concatenate([tile_buf[b * per + k] for k in range(per)], axis=1))
-        for k in range(per):
-            t = b * per + k
-            chain[t + shift] = chain[index_s[0, t]] + product[:, k * SIDE:(k + 1) * SIDE]
-        return carry
-
-    def tile_work(i):
-        tile_loads[i].wait()
-        step = blocks // CHUNKS
-        lax.fori_loop(i * step, (i + 1) * step, functools.partial(row_block, ahead[i]), 0)
-
-    first_loads[1].wait()
-    for i in order[:2]:
-        tile_work(i)
-    for k in range(HALO):
-        rim_out[0, k] = chain[k * per].astype(BF16)
-        rim_out[1, k] = chain[(blocks - HALO + k) * per + ahead[CHUNKS - 1]].astype(BF16)
-
-    pl.semaphore_wait(barrier, len(peers))
+
+    for copy in rim_loads:
+        copy.wait()
+    for k, b in enumerate(ends):
+        rim_out[k // HALO, k % HALO] = dot(grad_buf[b * SIDE:(b + 1) * SIDE, :].T, rim_tiles[k]).astype(BF16)
+
+    pl.semaphore_wait(barrier, len(near))
     sums = [
         remote(rim_out.at[0], rim_in.at[0], rim_send.at[0], rim_recv.at[0], down, c),
         remote(rim_out.at[1], rim_in.at[1], rim_send.at[1], rim_recv.at[1], up, c),
@@ -140,17 +133,26 @@
         copy.start()
     pair_feat = remote(feat, feat_buf.at[:, own_cols], pair_send.at[0], pair_recv.at[0], m, other)
     pair_feat.start()
-    for i in order[2:]:
+    pass_on(heard_1, 1, "xyz")
+    to_scalar.wait()
+    load_grad.wait()
+
+    for b in range(blocks):
+        span = pl.ds(b * SIDE, SIDE)
+        full_t[c, :, span] = grad_buf[span, :].T
+
+    def tile_work(i):
+        tile_loads[i].wait()
+        for b in range(i * blocks // CHUNKS, (i + 1) * blocks // CHUNKS):
+            product = dot(
+                full_t[c, :, pl.ds(b * SIDE, SIDE)],
+                jnp.concatenate([tile_buf[b * per + k] for k in range(per)], axis=1))
+            for k in range(per):
+                t = b * per + k
+                chain[t] = chain[index_s[0, t]] + product[:, k * SIDE:(k + 1) * SIDE]
+
+    for i in range(CHUNKS // 2):
         tile_work(i)
-
-    def column_block(b, value):
-        span = pl.ds(b * SIDE, SIDE)
-        hi = value.astype(BF16)
-        full_t[2 + c, :, span] = hi
-        low_t[:, span] = (value - hi.astype(F32)).astype(BF16)
-
-    for b in range(HALO, blocks - HALO):
-        column_block(b, chain[index_s[1, b]])
 
     share = SIDE // nx
     stage_x = [[], []]
@@ -168,7 +170,26 @@
 
     late_loads[0].wait()
     pair_feat.wait_recv()
+    hear(heard_1, "xyz")
+    pass_on(heard_2, 2, "yz")
     send_share(0, dot(full_t[c], feat_buf[...]))
+    for i in range(CHUNKS // 2, CHUNKS):
+        tile_work(i)
+
+    def column_block(b, value):
+        span = pl.ds(b * SIDE, SIDE)
+        hi = value.astype(BF16)
+        full_t[2 + c, :, span] = hi
+        low_t[:, span] = (value - hi.astype(F32)).astype(BF16)
+
+    for b in range(HALO, blocks - HALO):
+        column_block(b, chain[index_s[1, b]])
+
+    def product(low, high):
+        span = pl.ds(low, high - low)
+        return dot(full_t[2 + c, :, span], feat_buf[span, :]) + dot(low_t[:, span], feat_buf[span, :])
+
+    inner = product(rim, rows - rim)
     for copy in sums:
         copy.wait_recv()
     for k in range(HALO):
@@ -176,11 +197,13 @@
         column_block(b, chain[index_s[1, b]] + rim_in[0, k].astype(F32))
         b = HALO - 1 - k
         column_block(b, chain[index_s[1, b]] + rim_in[1, k].astype(F32))
-    send_share(1, dot(full_t[2 + c], feat_buf[...]) + dot(low_t[...], feat_buf[...]))
+    send_share(1, inner + product(0, rim) + product(rows - rim, rows))
     pair_grad = remote(full_t.at[c], full_t.at[c], pair_send.at[1], pair_recv.at[1], m, other)
     pair_grad.start()
     pair_sum = remote(full_t.at[2 + c], full_t.at[2 + c], pair_send.at[2], pair_recv.at[2], m, other)
     pair_sum.start()
+    hear(heard_2, "yz")
+    pass_on(heard_3, 2, "z")
     for copy in late_loads[1:]:
         copy.wait()
 
@@ -208,13 +231,13 @@
     weights = jnp.concatenate([w_buf[0], w_buf[1]], axis=1)
     wide = 2 * SIDE
 
-    def feature_part(i, carry):
-        span = pl.ds(pl.multiple_of(i * wide, wide), wide)
-        fgrad[span, :] = dot(weights, full_t[:, :, span].reshape(4 * SIDE, wide)).T
-        return carry
+    def feature_part(low, high):
+        for i in range(low, high):
+            span = pl.ds(i * wide, wide)
+            fgrad[span, :] = dot(weights, full_t[:, :, span].reshape(4 * SIDE, wide)).T
 
     halves = rows // wide // 2
-    lax.fori_loop(0, halves, feature_part, 0)
+    feature_part(0, halves)
 
     for yy in group_y:
         arrived(sum_y, recv_y.at[yy])
@@ -223,12 +246,15 @@
         total = total + got_y[yy]
     sum_y[...] = total
 
+    hear(heard_3, "z")
     stage_z = []
     for zz in group_z:
         stage_z.append(remote(sum_y, got_z.at[z], send_z.at[zz], recv_z.at[z], at(x, zz, y), c))
         stage_z[-1].start()
     got_z[z] = total
-    lax.fori_loop(halves, 2 * halves, feature_part, 0)
+    feature_part(halves, 2 * halves)
+    for copy in [pair_feat, pair_grad, pair_sum] + sums + stage_x[0] + stage_x[1] + stage_y:
+        copy.wait_send()
     for zz in group_z:
         arrived(sum_y, recv_z.at[zz])
     total = got_z[0]
@@ -249,6 +275,8 @@
             back.append(remote(
                 every.at[x, rows_of], every.at[x, rows_of], send_ax.at[xx, yy], recv_ax.at[x, yy], at(xx, z, y), c))
             back[-1].start()
+    for copy in stage_z + back[:ny + nx - 2]:
+        copy.wait_send()
     for yy in [y] + group_y[::-1]:
         rows_of = pl.ds(pl.multiple_of(yy * piece, piece), piece)
         for xx in group_ax:
@@ -259,7 +287,7 @@
             value = jnp.concatenate([every[q, base:base + share, :] for q in range(nx)], axis=0)
             wgrad[which, :, cc * SIDE:(cc + 1) * SIDE] = value.T
 
-    for copy in [pair_feat, pair_grad, pair_sum] + sums + stage_x[0] + stage_x[1] + stage_y + stage_z + back:
+    for copy in back[ny + nx - 2:]:
         copy.wait_send()
 
 
@@ -271,10 +299,12 @@
     share = SIDE // nx
     piece = 4 * share // ny
     dma = pltpu.SemaphoreType.DMA
+    anywhere = pl.BlockSpec(memory_space=pl.ANY)
+    heard = pltpu.SemaphoreType.REGULAR((3,))
     feature_grad, weight_grad = pl.pallas_call(
         functools.partial(kernel, torus),
         out_shape=(pltpu.VMEM((rows, columns), F32), pltpu.VMEM((2, columns, width), F32)),
-        in_specs=[pl.BlockSpec(memory_space=pl.ANY)] * 6,
+        in_specs=[anywhere] * 6,
         out_specs=(pl.BlockSpec(memory_space=pltpu.VMEM),) * 2,
         scratch_shapes=[
             pltpu.VMEM((count, SIDE, SIDE), BF16),
@@ -287,6 +317,7 @@
             pltpu.VMEM((count + 1, SIDE, SIDE), F32),
             pltpu.VMEM((4, SIDE, rows), BF16),
             pltpu.VMEM((SIDE, rows), BF16),
+            pltpu.VMEM((2 * HALO, SIDE, SIDE), BF16),
             pltpu.VMEM((2, HALO, SIDE, SIDE), BF16),
             pltpu.VMEM((2, HALO, SIDE, SIDE), BF16),
             pltpu.VMEM((2, 2, nx, share, SIDE), F32),
@@ -296,7 +327,8 @@
             pltpu.VMEM((piece, SIDE), F32),
             pltpu.VMEM((nz, piece, SIDE), F32),
             pltpu.VMEM((nx, 4 * share, SIDE), F32),
-            dma((6,)), dma((CHUNKS,)), dma((3,)), dma((3,)), dma((2,)), dma((2,)),
+            dma((12,)), dma((CHUNKS,)), dma((3,)), dma((3,)), dma((2,)), dma((2,)),
+            heard, heard, heard,
             dma((2, 2 * nx)), dma((2, 2 * nx)), dma((ny,)), dma((ny,)), dma((nz,)), dma((nz,)),
             dma((ny,)), dma((ny,)), dma((nx, ny)), dma((nx, ny)),
         ],

time: 50 us -> 47.9 us (0.958)
  Pallas kernels: 47.5 us -> 45.4 us
    pallas_call x1, Pallas kernels: 47.5 us -> 45.4 us  [body(): pl.pallas_call(functools.partial(kernel, torus), out_shape=(pltpu.VMEM((r...]
where the time goes in v3:
time: 47.9 us; the launch traced here: 47.7 us
  Pallas kernels  45.4 us (95%)
  local copies, waits for them, and re-layouts  1.69 us (4%)
  between operations  0.64 us (1%)
    pallas_call x1, Pallas kernels, body(): pl.pallas_call(functools.partial(kernel, torus), out_shape=(pltpu.VMEM((r...  45.4 us
    unnamed x1, local copies, waits for them, and re-layouts  0.97 us

profile of v3, /device:TPU:8, one launch (start us, length us, event | category | flops | bytes accessed | tf_op | source)
XLA Modules:
  0.0 47.7 jit_solution(8161767100638169861)
XLA Ops:
  0.6 45.4 %shard_map.85 = (f32[2048,128]{1,0:T(8,128)S(1)}, f32[2,128,256]{2,1,0:T(8,128)S(1)}) custom-call(bf16[2048,128]{1,0:T(8,128)(2,1)} %feat.1, bf16[2048,128]{1,0:T(8,128)(2,1)} %grad.1, bf16[64,128,128]{2,1,0:T(8,128)(2,1)} %tiles.1, s32[1,64]{1,0:T(1,128)} %bitcast.5, bf16[128,256]{1,0:T(8,128)(2,1)} %self_w.1, bf16[128,256]{1,0:T(8,128)(2,1)} %neigh_w.1), custom_call_target="tpu_custom_call" | custom-call | flops 1100000000 | bytes 4500000 | tf_op jit(solution)/shard_map/pallas_call | solution.py:304
  46.1 1.0 %copy.10 = f32[2048,128]{1,0:T(8,128)} copy(f32[2048,128]{1,0:T(8,128)S(1)} %get-tuple-element.9) | data formatting | bytes 2097152
  47.0 0.7 %slice_bitcast_fusion = (f32[128,256]{1,0:T(8,128)}, f32[128,256]{1,0:T(8,128)}) fusion(f32[2,128,256]{2,1,0:T(8,128)S(1)} %get-tuple-element.6), kind=kLoop, calls=%fused_computation | loop fusion | bytes 524288 | tf_op jit(solution)/shard_map/squeeze | solution.py:340

commit v4 on v3

--- a/solution.py
+++ b/solution.py
@@ -27,7 +27,7 @@
     chain, full_t, low_t, rim_tiles, rim_out, rim_in,
     part, got_x, sum_x, got_y, sum_y, got_z, every,
     load_sem, tile_sem, pair_send, pair_recv, rim_send, rim_recv,
-    heard_1, heard_2, heard_3, send_x, recv_x, send_y, recv_y, send_z, recv_z, send_ay, recv_ay, send_ax, recv_ax,
+    heard_1, heard_2, heard_3, send_x, recv_x, send_y, recv_y, send_z, recv_z, send_back, recv_back,
 ):
     nx, nz, ny = torus
     n = nx * nz * ny
@@ -49,7 +49,6 @@
     group_x = [((x + k) % nx, (c + j) % 2) for k in far_first(nx) + [0] for j in ((0, 1) if k else (1,))]
     group_y = [(y + k) % ny for k in far_first(ny)]
     group_z = [(z + k) % nz for k in far_first(nz)]
-    group_ax = [(x + k) % nx for k in far_first(nx)]
 
     def remote(src, dst, send, recv, blk, rep):
         return pltpu.make_async_remote_copy(
@@ -260,34 +259,26 @@
     total = got_z[0]
     for zz in range(1, nz):
         total = total + got_z[zz]
-    every[x, own_piece, :] = total
-
+    every[x, own_piece, :] = total.astype(BF16)
+
+    plane = [(i, j) for i in range(nx) for j in range(ny) if i or j]
+    plane = [((x + i) % nx, (y + j) % ny) for i, j in sorted(plane, key=lambda p: -min(p[0], nx - p[0]) - min(p[1], ny - p[1]))]
     back = []
-    for yy in group_y:
+    for xx, yy in plane:
         back.append(remote(
-            every.at[x, own_piece], every.at[x, own_piece], send_ay.at[yy], recv_ay.at[y], at(x, z, yy), c))
+            every.at[x, own_piece], every.at[x, own_piece], send_back.at[xx, yy], recv_back.at[x, y], at(xx, z, yy), c))
         back[-1].start()
-    for yy in [y] + group_y[::-1]:
-        rows_of = pl.ds(pl.multiple_of(yy * piece, piece), piece)
-        if yy is not y:
-            arrived(every.at[x, rows_of], recv_ay.at[yy])
-        for xx in group_ax:
-            back.append(remote(
-                every.at[x, rows_of], every.at[x, rows_of], send_ax.at[xx, yy], recv_ax.at[x, yy], at(xx, z, y), c))
-            back[-1].start()
-    for copy in stage_z + back[:ny + nx - 2]:
+    for copy in stage_z:
         copy.wait_send()
-    for yy in [y] + group_y[::-1]:
-        rows_of = pl.ds(pl.multiple_of(yy * piece, piece), piece)
-        for xx in group_ax:
-            arrived(every.at[xx, rows_of], recv_ax.at[xx, yy])
+    for xx, yy in plane[::-1]:
+        arrived(every.at[xx, pl.ds(pl.multiple_of(yy * piece, piece), piece)], recv_back.at[xx, yy])
     for which in range(2):
         for cc in range(2):
             base = (2 * cc + which) * share
             value = jnp.concatenate([every[q, base:base + share, :] for q in range(nx)], axis=0)
-            wgrad[which, :, cc * SIDE:(cc + 1) * SIDE] = value.T
-
-    for copy in back[ny + nx - 2:]:
+            wgrad[which, :, cc * SIDE:(cc + 1) * SIDE] = value.astype(F32).T
+
+    for copy in back:
         copy.wait_send()
 
 
@@ -326,11 +317,11 @@
             pltpu.VMEM((ny, piece, SIDE), F32),
             pltpu.VMEM((piece, SIDE), F32),
             pltpu.VMEM((nz, piece, SIDE), F32),
-            pltpu.VMEM((nx, 4 * share, SIDE), F32),
+            pltpu.VMEM((nx, 4 * share, SIDE), BF16),
             dma((12,)), dma((CHUNKS,)), dma((3,)), dma((3,)), dma((2,)), dma((2,)),
             heard, heard, heard,
             dma((2, 2 * nx)), dma((2, 2 * nx)), dma((ny,)), dma((ny,)), dma((nz,)), dma((nz,)),
-            dma((ny,)), dma((ny,)), dma((nx, ny)), dma((nx, ny)),
+            dma((nx, ny)), dma((nx, ny)),
         ],
         compiler_params=pltpu.CompilerParams(
             collective_id=0, has_side_effects=True, vmem_limit_bytes=VMEM_BYTES

time: 47.9 us -> 45.2 us (0.944)
  Pallas kernels: 45.4 us -> 42.7 us
    pallas_call x1, Pallas kernels: 45.4 us -> 42.7 us  [body(): pl.pallas_call(functools.partial(kernel, torus), out_shape=(pltpu.VMEM((r...]
where the time goes in v4:
time: 45.2 us; the launch traced here: 45 us
  Pallas kernels  42.7 us (94%)
  local copies, waits for them, and re-layouts  1.69 us (4%)
  between operations  0.64 us (1%)
    pallas_call x1, Pallas kernels, body(): pl.pallas_call(functools.partial(kernel, torus), out_shape=(pltpu.VMEM((r...  42.7 us
    unnamed x1, local copies, waits for them, and re-layouts  0.97 us

profile of v4, /device:TPU:8, one launch (start us, length us, event | category | flops | bytes accessed | tf_op | source)
XLA Modules:
  0.0 45.0 jit_solution(16535647328905437025)
XLA Ops:
  0.6 42.7 %shard_map.85 = (f32[2048,128]{1,0:T(8,128)S(1)}, f32[2,128,256]{2,1,0:T(8,128)S(1)}) custom-call(bf16[2048,128]{1,0:T(8,128)(2,1)} %feat.1, bf16[2048,128]{1,0:T(8,128)(2,1)} %grad.1, bf16[64,128,128]{2,1,0:T(8,128)(2,1)} %tiles.1, s32[1,64]{1,0:T(1,128)} %bitcast.5, bf16[128,256]{1,0:T(8,128)(2,1)} %self_w.1, bf16[128,256]{1,0:T(8,128)(2,1)} %neigh_w.1), custom_call_target="tpu_custom_call" | custom-call | flops 1100000000 | bytes 4500000 | tf_op jit(solution)/shard_map/pallas_call | solution.py:295
  43.3 1.0 %copy.10 = f32[2048,128]{1,0:T(8,128)} copy(f32[2048,128]{1,0:T(8,128)S(1)} %get-tuple-element.9) | data formatting | bytes 2097152
  44.3 0.7 %slice_bitcast_fusion = (f32[128,256]{1,0:T(8,128)}, f32[128,256]{1,0:T(8,128)}) fusion(f32[2,128,256]{2,1,0:T(8,128)S(1)} %get-tuple-element.6), kind=kLoop, calls=%fused_computation | loop fusion | bytes 524288 | tf_op jit(solution)/shard_map/squeeze | solution.py:331

commit v5 on v4

--- a/solution.py
+++ b/solution.py
@@ -63,8 +63,9 @@
         pl.semaphore_signal(sem, inc=1, device_id={"blk": blk, "rep": rep}, device_id_type=pl.DeviceIdType.MESH)
 
     barrier = pltpu.get_barrier_semaphore()
-    near = [(at(x, (z + k) % nz, y), c) for k in (1, nz - 1)] + [(at(x, z, (y + k) % ny), c) for k in (1, ny - 1)]
-    near += [(at((x + k) % nx, z, y), cc) for k in (1, nx - 1) for cc in (c, other)] + [(m, other), (up, c), (down, c)]
+    near = [(up, c), (down, c)]
+    near += [(at(x, (z + k) % nz, y), c) for k in (1, nz - 1)] + [(at(x, z, (y + k) % ny), c) for k in (1, ny - 1)]
+    near += [(at((x + k) % nx, z, y), cc) for k in (1, nx - 1) for cc in (c, other)] + [(m, other)]
     for blk, rep in near:
         signal(barrier, blk, rep)
 
@@ -184,11 +185,14 @@
     for b in range(HALO, blocks - HALO):
         column_block(b, chain[index_s[1, b]])
 
-    def product(low, high):
-        span = pl.ds(low, high - low)
-        return dot(full_t[2 + c, :, span], feat_buf[span, :]) + dot(low_t[:, span], feat_buf[span, :])
-
-    inner = product(rim, rows - rim)
+    def product(*spans):
+        spans = [pl.ds(low, high - low) for low, high in spans]
+        right = jnp.concatenate([feat_buf[span, :] for span in spans], axis=0)
+        high_part = jnp.concatenate([full_t[2 + c, :, span] for span in spans], axis=1)
+        low_part = jnp.concatenate([low_t[:, span] for span in spans], axis=1)
+        return dot(high_part, right) + dot(low_part, right)
+
+    inner = product((rim, rows - rim))
     for copy in sums:
         copy.wait_recv()
     for k in range(HALO):
@@ -196,7 +200,7 @@
         column_block(b, chain[index_s[1, b]] + rim_in[0, k].astype(F32))
         b = HALO - 1 - k
         column_block(b, chain[index_s[1, b]] + rim_in[1, k].astype(F32))
-    send_share(1, inner + product(0, rim) + product(rows - rim, rows))
+    send_share(1, inner + product((0, rim), (rows - rim, rows)))
     pair_grad = remote(full_t.at[c], full_t.at[c], pair_send.at[1], pair_recv.at[1], m, other)
     pair_grad.start()
     pair_sum = remote(full_t.at[2 + c], full_t.at[2 + c], pair_send.at[2], pair_recv.at[2], m, other)
@@ -225,19 +229,6 @@
         stage_y[-1].start()
     got_y[y] = sum_x[own_piece, :]
 
-    pair_grad.wait_recv()
-    pair_sum.wait_recv()
-    weights = jnp.concatenate([w_buf[0], w_buf[1]], axis=1)
-    wide = 2 * SIDE
-
-    def feature_part(low, high):
-        for i in range(low, high):
-            span = pl.ds(i * wide, wide)
-            fgrad[span, :] = dot(weights, full_t[:, :, span].reshape(4 * SIDE, wide)).T
-
-    halves = rows // wide // 2
-    feature_part(0, halves)
-
     for yy in group_y:
         arrived(sum_y, recv_y.at[yy])
     total = got_y[0]
@@ -251,7 +242,17 @@
         stage_z.append(remote(sum_y, got_z.at[z], send_z.at[zz], recv_z.at[z], at(x, zz, y), c))
         stage_z[-1].start()
     got_z[z] = total
-    feature_part(halves, 2 * halves)
+    pair_grad.wait_recv()
+    pair_sum.wait_recv()
+    weights = jnp.concatenate([w_buf[0], w_buf[1]], axis=1)
+    wide = 2 * SIDE
+
+    def feature_part(low, high):
+        for i in range(low, high):
+            span = pl.ds(i * wide, wide)
+            fgrad[span, :] = dot(weights, full_t[:, :, span].reshape(4 * SIDE, wide)).T
+
+    feature_part(0, rows // wide)
     for copy in [pair_feat, pair_grad, pair_sum] + sums + stage_x[0] + stage_x[1] + stage_y:
         copy.wait_send()
     for zz in group_z:
@@ -280,6 +281,22 @@
 
     for copy in back:
         copy.wait_send()
+
+
+def write(feature_in, weight_in, feature_out, self_out, neighbor_out, sem):
+    part = feature_in.shape[0] // 4
+    copies = [
+        pltpu.make_async_copy(feature_in.at[pl.ds(i * part, part)], feature_out.at[pl.ds(i * part, part)], sem.at[i])
+        for i in range(4)
+    ]
+    copies += [
+        pltpu.make_async_copy(weight_in.at[0], self_out, sem.at[4]),
+        pltpu.make_async_copy(weight_in.at[1], neighbor_out, sem.at[5]),
+    ]
+    for copy in copies:
+        copy.start()
+    for copy in copies:
+        copy.wait()
 
 
 def body(torus, features, out_grad, block_tiles, block_cols, self_weight, neighbor_weight):
@@ -328,7 +345,21 @@
         ),
         cost_estimate=pl.CostEstimate(flops=1100000000, bytes_accessed=4500000, transcendentals=0),
     )(features, out_grad, block_tiles, block_cols.reshape(1, count), self_weight, neighbor_weight)
-    return feature_grad, weight_grad[0], weight_grad[1]
+    feature_grad = pltpu.with_memory_space_constraint(feature_grad, pltpu.VMEM)
+    weight_grad = pltpu.with_memory_space_constraint(weight_grad, pltpu.VMEM)
+    return pl.pallas_call(
+        write,
+        out_shape=(
+            jax.ShapeDtypeStruct((rows, columns), F32),
+            jax.ShapeDtypeStruct((columns, width), F32),
+            jax.ShapeDtypeStruct((columns, width), F32),
+        ),
+        in_specs=[pl.BlockSpec(memory_space=pltpu.VMEM)] * 2,
+        out_specs=(anywhere,) * 3,
+        scratch_shapes=[dma((6,))],
+        compiler_params=pltpu.CompilerParams(vmem_limit_bytes=VMEM_BYTES),
+        cost_estimate=pl.CostEstimate(flops=0, bytes_accessed=2600000, transcendentals=0),
+    )(feature_grad, weight_grad)
 
 
 def solution(mesh):

time: 45.2 us -> 44.5 us (0.985)
  local copies, waits for them, and re-layouts: 1.69 us -> 0 us
  Pallas kernels: 42.7 us -> 43.8 us
    pallas_call x0 -> x1, Pallas kernels: none -> 1.1 us  [body(): pl.pallas_call(write, out_shape=(jax.ShapeDtypeStruct((rows, columns), F3...]
    unnamed x1 -> x0, local copies, waits for them, and re-layouts: 0.97 us -> none
    squeeze x1 -> x0, local copies, waits for them, and re-layouts: 0.71 us -> none  [body(): return (feature_grad, weight_grad[0], weight_grad[1])]
where the time goes in v5:
time: 44.5 us; the launch traced here: 44.4 us
  Pallas kernels  43.8 us (98%)
  between operations  0.64 us (1%)
    pallas_call x1, Pallas kernels, body(): pl.pallas_call(functools.partial(kernel, torus), out_shape=(pltpu.VMEM((r...  42.7 us
    pallas_call x1, Pallas kernels, body(): pl.pallas_call(write, out_shape=(jax.ShapeDtypeStruct((rows, columns), F3...  1.1 us

profile of v5, /device:TPU:8, one launch (start us, length us, event | category | flops | bytes accessed | tf_op | source)
XLA Modules:
  0.0 44.4 jit_solution(16141629659138924651)
XLA Ops:
  0.6 42.7 %shard_map.85 = (f32[2048,128]{1,0:T(8,128)S(1)}, f32[2,128,256]{2,1,0:T(8,128)S(1)}) custom-call(bf16[2048,128]{1,0:T(8,128)(2,1)} %feat.1, bf16[2048,128]{1,0:T(8,128)(2,1)} %grad.1, bf16[64,128,128]{2,1,0:T(8,128)(2,1)} %tiles.1, s32[1,64]{1,0:T(1,128)} %bitcast.1, bf16[128,256]{1,0:T(8,128)(2,1)} %self_w.1, bf16[128,256]{1,0:T(8,128)(2,1)} %neigh_w.1), custom_call_target="tpu_custom_call" | custom-call | flops 1100000000 | bytes 4500000 | tf_op jit(solution)/shard_map/pallas_call | solution.py:312
  43.3 1.1 %shard_map.86 = (f32[2048,128]{1,0:T(8,128)}, f32[128,256]{1,0:T(8,128)}, f32[128,256]{1,0:T(8,128)}) custom-call(f32[2048,128]{1,0:T(8,128)S(1)} %get-tuple-element.5.feature_in, f32[2,128,256]{2,1,0:T(8,128)S(1)} %get-tuple-element.6.weight_in), custom_call_target="tpu_custom_call" | custom-call | bytes 2600000 | tf_op jit(solution)/shard_map/pallas_call | solution.py:350

commit v6 on v5

--- a/solution.py
+++ b/solution.py
@@ -173,6 +173,8 @@
     hear(heard_1, "xyz")
     pass_on(heard_2, 2, "yz")
     send_share(0, dot(full_t[c], feat_buf[...]))
+    pair_grad = remote(full_t.at[c], full_t.at[c], pair_send.at[1], pair_recv.at[1], m, other)
+    pair_grad.start()
     for i in range(CHUNKS // 2, CHUNKS):
         tile_work(i)
 
@@ -201,10 +203,6 @@
         b = HALO - 1 - k
         column_block(b, chain[index_s[1, b]] + rim_in[1, k].astype(F32))
     send_share(1, inner + product((0, rim), (rows - rim, rows)))
-    pair_grad = remote(full_t.at[c], full_t.at[c], pair_send.at[1], pair_recv.at[1], m, other)
-    pair_grad.start()
-    pair_sum = remote(full_t.at[2 + c], full_t.at[2 + c], pair_send.at[2], pair_recv.at[2], m, other)
-    pair_sum.start()
     hear(heard_2, "yz")
     pass_on(heard_3, 2, "z")
     for copy in late_loads[1:]:
@@ -227,6 +225,8 @@
             sum_x.at[pl.ds(pl.multiple_of(yy * piece, piece), piece)], got_y.at[y],
             send_y.at[yy], recv_y.at[y], at(x, z, yy), c))
         stage_y[-1].start()
+    pair_sum = remote(full_t.at[2 + c], full_t.at[2 + c], pair_send.at[2], pair_recv.at[2], m, other)
+    pair_sum.start()
     got_y[y] = sum_x[own_piece, :]
 
     for yy in group_y:

time: 44.5 us -> 44.5 us (level)
  no operation moved by 1% of the time
where the time goes in v6:
time: 44.5 us; the launch traced here: 44.4 us
  Pallas kernels  43.8 us (98%)
  between operations  0.64 us (1%)
    pallas_call x1, Pallas kernels, body(): pl.pallas_call(functools.partial(kernel, torus), out_shape=(pltpu.VMEM((r...  42.7 us
    pallas_call x1, Pallas kernels, body(): pl.pallas_call(write, out_shape=(jax.ShapeDtypeStruct((rows, columns), F3...  1.1 us

profile of v6, /device:TPU:8, one launch (start us, length us, event | category | flops | bytes accessed | tf_op | source)
XLA Modules:
  0.0 44.4 jit_solution(17366421649386324085)
XLA Ops:
  0.6 42.7 %shard_map.85 = (f32[2048,128]{1,0:T(8,128)S(1)}, f32[2,128,256]{2,1,0:T(8,128)S(1)}) custom-call(bf16[2048,128]{1,0:T(8,128)(2,1)} %feat.1, bf16[2048,128]{1,0:T(8,128)(2,1)} %grad.1, bf16[64,128,128]{2,1,0:T(8,128)(2,1)} %tiles.1, s32[1,64]{1,0:T(1,128)} %bitcast.1, bf16[128,256]{1,0:T(8,128)(2,1)} %self_w.1, bf16[128,256]{1,0:T(8,128)(2,1)} %neigh_w.1), custom_call_target="tpu_custom_call" | custom-call | flops 1100000000 | bytes 4500000 | tf_op jit(solution)/shard_map/pallas_call | solution.py:312
  43.3 1.1 %shard_map.86 = (f32[2048,128]{1,0:T(8,128)}, f32[128,256]{1,0:T(8,128)}, f32[128,256]{1,0:T(8,128)}) custom-call(f32[2048,128]{1,0:T(8,128)S(1)} %get-tuple-element.5.feature_in, f32[2,128,256]{2,1,0:T(8,128)S(1)} %get-tuple-element.6.weight_in), custom_call_target="tpu_custom_call" | custom-call | bytes 2600000 | tf_op jit(solution)/shard_map/pallas_call | solution.py:350
